TPU v7x, 32 devices: a whole 2x2x4 slice. The times are simulated.
32 devices in a mesh: seq: 8 (over z, x), head: 4 (over y, core).
Axes of the slice: x: 2, y: 2, z: 4, core: 2. Of those that a mesh axis runs over, the one named last changes fastest.
Arguments:
- queries: bfloat16 [16, 4096, 128], P(None, ('seq', 'head')), may hold values from -0.5390625 to 0.5390625
- keys: bfloat16 [16, 4096, 128], P(None, ('seq', 'head')), may hold values from -0.5390625 to 0.5390625
- values: bfloat16 [16, 4096, 128], P(None, ('seq', 'head')), may hold values from -24 to 24
- out_grad: bfloat16 [16, 4096, 128], P(None, ('seq', 'head')), may hold values from -6 to 6
- regular: float32 [16, 128], P('head'), may hold values from 0.25 to 4
Outputs:
- output: bfloat16 [16, 4096, 128], P(None, ('seq', 'head'))
- query_grad: bfloat16 [16, 4096, 128], P(None, ('seq', 'head'))
- key_grad: bfloat16 [16, 4096, 128], P(None, ('seq', 'head'))
- value_grad: bfloat16 [16, 4096, 128], P(None, ('seq', 'head'))
All inputs are finite; a program needn't handle non-finite values.
Results may differ from a plain program's by a relative error of at most 0.001.
Values may be sent and summed in bfloat16 or wider, within the bound.
A program may use at most 64 MiB of HBM per device.

v0:
```python
from functools import partial

import jax
import jax.numpy as jnp
from jax import lax
from jax.sharding import PartitionSpec as P

GROUP = 128


def exact_einsum(form, left, right):
    return jnp.einsum(form, left, right, precision=lax.Precision.HIGHEST)


def group_output(query_rows, key_rows, value_rows, gram_in, state_in, causal):
    eye_dim = jnp.broadcast_to(jnp.eye(gram_in.shape[-1], dtype=jnp.float32), gram_in.shape)
    low_gram = jnp.linalg.cholesky(gram_in)
    half_inv = lax.linalg.triangular_solve(low_gram, eye_dim, left_side=True, lower=True)
    inverse = lax.linalg.triangular_solve(
        low_gram, half_inv, left_side=True, lower=True, transpose_a=True
    )
    key_inv = exact_einsum("...cd,...de->...ce", key_rows, inverse)
    inner_mat = exact_einsum("...ce,...te->...ct", key_inv, key_rows)
    eye_rows = jnp.eye(causal.shape[0], dtype=jnp.float32)
    low_mix = jnp.linalg.cholesky(inner_mat + eye_rows)
    right_side = exact_einsum("...ce,...te->...ct", key_inv, query_rows)
    first_pass = (
        lax.linalg.triangular_solve(low_mix, right_side, left_side=True, lower=True) * causal
    )
    second_pass = (
        lax.linalg.triangular_solve(
            low_mix, first_pass, left_side=True, lower=True, transpose_a=True
        )
        * causal
    )
    solved = exact_einsum("...de,...te->...dt", inverse, query_rows) - exact_einsum(
        "...cd,...ct->...dt", key_inv, second_pass
    )
    scores = exact_einsum("...cd,...dt->...ct", key_rows, solved) * causal
    return exact_einsum("...ed,...dt->...te", state_in, solved) + exact_einsum(
        "...ce,...ct->...te", value_rows, scores
    )


def on_device(queries, keys, values, out_grad, regular):
    queries, keys, values, out_grad = (
        lax.all_to_all(queries, "head", split_axis=0, concat_axis=1, tiled=True),
        lax.all_to_all(keys, "head", split_axis=0, concat_axis=1, tiled=True),
        lax.all_to_all(values, "head", split_axis=0, concat_axis=1, tiled=True),
        lax.all_to_all(out_grad, "head", split_axis=0, concat_axis=1, tiled=True),
    )
    head_count, token_count, feature = keys.shape
    group_len = GROUP
    block_count = token_count // group_len
    block_shape = (head_count, block_count, group_len, feature)
    key_blocks = keys.reshape(block_shape)
    value_blocks = values.reshape(block_shape)
    grams = jnp.einsum(
        "hncd,hnce->hnde", key_blocks, key_blocks, preferred_element_type=jnp.float32
    )
    states = jnp.einsum(
        "hnce,hncd->hned", value_blocks, key_blocks, preferred_element_type=jnp.float32
    )
    zero_block = jnp.zeros_like(grams[:, :1])
    gram_local = jnp.concatenate([zero_block, jnp.cumsum(grams, axis=1)[:, :-1]], axis=1)
    state_local = jnp.concatenate([zero_block, jnp.cumsum(states, axis=1)[:, :-1]], axis=1)
    total_gram = jnp.sum(grams, axis=1)
    total_state = jnp.sum(states, axis=1)
    every_gram, every_state = (
        lax.all_gather(total_gram[None], "seq", axis=0, tiled=True),
        lax.all_gather(total_state[None], "seq", axis=0, tiled=True),
    )
    rank = lax.axis_index("seq")
    below = (jnp.arange(every_gram.shape[0]) < rank).astype(jnp.float32)
    lower_gram = exact_einsum("s,shde->hde", below, every_gram)
    lower_state = exact_einsum("s,shde->hde", below, every_state)
    base = regular[:, :, None] * jnp.eye(feature, dtype=jnp.float32)
    gram_in = base[:, None] + (lower_gram[:, None] + gram_local)
    state_in = lower_state[:, None] + state_local
    positions = jnp.arange(group_len)
    causal = (positions[:, None] <= positions[None, :]).astype(jnp.float32)
    query_full = queries.reshape(block_shape).astype(jnp.float32)
    key_full = key_blocks.astype(jnp.float32)
    value_full = value_blocks.astype(jnp.float32)
    grad_full = out_grad.reshape(block_shape).astype(jnp.float32)
    result, pull = jax.vjp(
        partial(group_output, causal=causal), query_full, key_full, value_full, gram_in, state_in
    )
    dq_part, dk_part, dv_part, dgram_part, dstate_part = pull(grad_full)
    gram_incl = jnp.flip(jnp.cumsum(jnp.flip(dgram_part, 1), axis=1), 1)
    state_incl = jnp.flip(jnp.cumsum(jnp.flip(dstate_part, 1), axis=1), 1)
    gram_after = jnp.concatenate([gram_incl[:, 1:], zero_block], axis=1)
    state_after = jnp.concatenate([state_incl[:, 1:], zero_block], axis=1)
    grad_gram_total = gram_incl[:, 0]
    grad_state_total = state_incl[:, 0]
    every_dgram, every_dstate = (
        lax.all_gather(grad_gram_total[None], "seq", axis=0, tiled=True),
        lax.all_gather(grad_state_total[None], "seq", axis=0, tiled=True),
    )
    rank_back = lax.axis_index("seq")
    above = (jnp.arange(every_dgram.shape[0]) > rank_back).astype(jnp.float32)
    upper_gram = exact_einsum("s,shde->hde", above, every_dgram)
    upper_state = exact_einsum("s,shde->hde", above, every_dstate)
    gram_later = upper_gram[:, None] + gram_after
    state_later = upper_state[:, None] + state_after
    sym_later = gram_later + jnp.swapaxes(gram_later, -1, -2)
    dk_total = (
        dk_part
        + exact_einsum("hnde,hnce->hncd", sym_later, key_full)
        + exact_einsum("hned,hnce->hncd", state_later, value_full)
    )
    dv_total = dv_part + exact_einsum("hned,hncd->hnce", state_later, key_full)
    flat_shape = (head_count, token_count, feature)
    output = result.reshape(flat_shape).astype(jnp.bfloat16)
    query_grad = dq_part.reshape(flat_shape).astype(jnp.bfloat16)
    key_grad = dk_total.reshape(flat_shape).astype(jnp.bfloat16)
    value_grad = dv_total.reshape(flat_shape).astype(jnp.bfloat16)
    return (
        lax.all_to_all(output, "head", split_axis=1, concat_axis=0, tiled=True),
        lax.all_to_all(query_grad, "head", split_axis=1, concat_axis=0, tiled=True),
        lax.all_to_all(key_grad, "head", split_axis=1, concat_axis=0, tiled=True),
        lax.all_to_all(value_grad, "head", split_axis=1, concat_axis=0, tiled=True),
    )


def solution(mesh):
    placed = (
        P(None, ("seq", "head"), None),
        P(None, ("seq", "head"), None),
        P(None, ("seq", "head"), None),
        P(None, ("seq", "head"), None),
        P("head", None),
    )
    return jax.shard_map(
        on_device,
        mesh=mesh,
        in_specs=placed,
        out_specs=(
            P(None, ("seq", "head"), None),
            P(None, ("seq", "head"), None),
            P(None, ("seq", "head"), None),
            P(None, ("seq", "head"), None),
        ),
        check_vma=False,
    )
```

profile of v0, /device:TPU:0, one launch (start us, length us, event | category | flops | bytes accessed | tf_op | source)
XLA Modules:
  0.0 1300.4 jit_solution(8068362834263849749)
XLA Ops:
  7.2 13.1 %all_to_all.132 = bf16[16,128,128]{2,1,0:T(8,128)(2,1)S(1)} all-to-all(bf16[16,128,128]{2,1,0:T(8,128)(2,1)} %param.18), channel_id=1, replica_groups=mesh['seq'=8,'head'=4] {'head'}, dimensions={0} | all-to-all | bytes 1048576 | tf_op jit(solution)/shard_map/all_to_all | solution.py:48
  21.4 3.5 all-to-all-start.2
  26.9 6.8 all-to-all-done.2
  33.7 3.5 all-to-all-start.4
  39.9 2.3 slice.47
  46.0 3.5 all-to-all-start.1
  53.1 18.7 %all-gather.9.cloned.1.call-done = f32[32,128,128]{2,1,0:T(8,128)} async-done(((f32[4,128,128]{2,1,0:T(8,128)}), f32[32,128,128]{2,1,0:T(8,128)}) %all-gather.9.cloned.1.call-update) | async-done | bytes 2097168 | tf_op jit(solution)/shard_map/all_gather | solution.py:70
  71.8 3.8 fusion.6
  79.5 188.3 %custom-call.27 = f32[4,4,128,128]{3,2,1,0:T(8,128)S(1)} custom-call(f32[4,4,128,128]{3,2,1,0:T(8,128)} %fusion.59), custom_call_target="Cholesky" | custom-call | tf_op jit(solution)/shard_map/jvp(jit(cholesky))/cholesky | solution.py:17
  270.0 157.8 %custom-call.29 = f32[4,4,1,128,128]{3,4,2,1,0:T(8,128)S(1)} custom-call(f32[4,4,1,128,128]{4,3,2,1,0:T(8,128)S(1)} %get-tuple-element.36), custom_call_target="InvertDiagBlocksLowerTriangular" | custom-call | tf_op jit(solution)/shard_map/jvp()/triangular_solve/custom-call.0 | solution.py:19
  431.8 2.3 fusion.77
  434.1 2.0 fusion.75
  437.7 3.9 fusion.4
  443.6 2.8 convolution_multiply_fusion.1
  448.0 2.4 fusion.50
  450.3 188.3 %custom-call.30 = f32[4,4,128,128]{3,2,1,0:T(8,128)S(1)} custom-call(f32[4,4,128,128]{3,2,1,0:T(8,128)} %fusion.50), custom_call_target="Cholesky" | custom-call | tf_op jit(solution)/shard_map/jvp(jit(cholesky))/cholesky | solution.py:25
  640.4 158.0 %custom-call.32 = f32[4,4,1,128,128]{3,4,2,1,0:T(8,128)S(1)} custom-call(f32[4,4,1,128,128]{4,3,2,1,0:T(8,128)} %get-tuple-element.38), custom_call_target="InvertDiagBlocksLowerTriangular" | custom-call | tf_op jit(solution)/shard_map/jvp()/triangular_solve/custom-call.0 | solution.py:31
  798.4 3.1 fusion.46
  804.6 3.3 fusion.160
  807.9 3.3 fusion.62
  811.2 3.3 fusion.161
  814.5 2.2 fusion.44
  816.7 159.0 %custom-call.37 = f32[4,4,1,128,128]{3,4,2,1,0:T(8,128)} custom-call(f32[4,4,1,128,128]{4,3,2,1,0:T(8,128)} %get-tuple-element.37), custom_call_target="InvertDiagBlocksLowerTriangular" | custom-call | tf_op jit(solution)/shard_map/transpose(jvp(jit(cholesky)))/triangular_solve/custom-call.0 | solution.py:25
  975.7 2.8 convolution_subtract_fusion
  981.2 2.3 rev.10
  986.8 2.5 fusion.18
  991.3 1.9 fusion.13
  994.4 2.3 fusion.37
  1002.0 2.3 convolution_add_fusion.4
  1007.8 158.8 %custom-call.42 = f32[4,4,1,128,128]{3,4,2,1,0:T(8,128)} custom-call(f32[4,4,1,128,128]{4,3,2,1,0:T(8,128)} %get-tuple-element.35), custom_call_target="InvertDiagBlocksLowerTriangular" | custom-call | tf_op jit(solution)/shard_map/transpose(jvp(jit(cholesky)))/triangular_solve/custom-call.0 | solution.py:17
  1166.6 1.9 convolution_add_fusion.1
  1168.6 1.9 fusion.51
  1170.5 2.3 fusion.162
  1172.8 2.3 fusion.163
  1178.3 1.9 fusion.9
  1181.4 3.7 fusion.31
  1185.1 2.5 copy.256
  1187.7 2.7 fusion.30
  1190.4 2.5 copy.257
  1192.9 2.7 bitcast_add_fusion.2
  1195.6 2.3 rev.9
  1200.9 2.2 slice.51
  1203.1 2.1 slice.49
  1211.0 4.2 all-to-all-start.3
  1215.1 2.1 slice.45
  1217.2 3.2 fusion.158
  1220.4 1.9 fusion.26
  1223.5 2.1 slice.42
  1225.6 4.1 fusion.159
  1229.7 2.9 convolution_add_fusion.5
  1232.6 3.8 fusion
  1236.6 12.2 all-gather.13.cloned.1.call-done
  1248.8 4.1 fusion.2
  1255.1 4.2 all-to-all-start.5
  1261.7 2.5 copy.258
  1264.2 3.5 convolution_bitcast_fusion.5
  1268.2 3.5 all-to-all-start.7
  1271.7 2.5 convolution_bitcast_fusion.3
  1274.2 2.3 fusion.28
  1277.8 2.8 all-to-all-done.7
  1280.5 3.5 all-to-all-start.6
  1284.0 1.9 copy.218
  1285.9 1.9 copy.231
  1288.8 4.0 all-to-all-done.6
  (191 shorter events, 73.6 us)
Async XLA Ops:
  7.2 64.6 %all-gather.9.cloned.1.call-start = ((), (), s32[]{:S(2)}) async-start(), calls=%async_computation.8 | async-start | bytes 2359296 | tf_op jit(solution)/shard_map/all_gather | solution.py:70
  20.3 6.6 copy-start.53
  21.4 12.3 all-to-all-start.2
  33.7 12.3 all-to-all-start.4
  37.2 400.5 %all-gather.11.cloned.1.call-start = ((), (), s32[]{:S(2)}) async-start(), calls=%async_computation.9 | async-start | bytes 2359296 | tf_op jit(solution)/shard_map/all_gather | solution.py:71
  39.9 9.9 copy-start.29
  46.0 7.1 copy-start.12
  46.0 385.8 %all-to-all-start.1 = ((bf16[16,128,128]{2,1,0:T(8,128)(2,1)}), bf16[16,128,128]{2,1,0:T(8,128)(2,1)S(1)}, u32[]{:S(2)}, u32[]{:S(2)}) async-start(bf16[16,128,128]{2,1,0:T(8,128)(2,1)} %param.17), calls=%async_computation.1 | async-start | bytes 1048576 | tf_op jit(solution)/shard_map/all_to_all | solution.py:47
  49.5 1183.1 %all-gather.15.cloned.1.call-start = ((), (), s32[]{:S(2)}) async-start(), calls=%async_computation.11 | async-start | bytes 2359296 | tf_op jit(solution)/shard_map/all_gather | solution.py:98
  50.3 1.0 copy-start.21
  267.8 2.2 copy-start.40
  268.8 160.8 %copy-start.54 = (pred[4,4]{1,0:T(4,128)(4,1)}, pred[4,4]{1,0:T(4,128)(4,1)S(1)}, u32[]{:S(2)}) copy-start(pred[4,4]{1,0:T(4,128)(4,1)S(1)} %compare_reduce_fusion.1) | copy-start | bytes 52
  427.8 1.9 copy-start.7
  429.6 1.2 copy-start.18
  430.8 3.3 copy-start
  436.1 5.5 copy-start.13
  436.1 5.5 copy-start.31
  437.7 3.9 copy-start.37
  441.6 1.1 copy-start.47
  442.7 1.0 copy-start.2
  443.6 2.8 copy-start.26
  448.0 190.7 %copy-start.51 = (pred[128,128]{1,0:T(8,128)(4,1)S(1)}, pred[128,128]{1,0:T(8,128)(4,1)}, u32[]{:S(2)}) copy-start(pred[128,128]{1,0:T(8,128)(4,1)} %iota_compare_fusion.3) | copy-start | bytes 49156
  638.6 1.8 copy-start.43
  801.5 1.2 copy-start.17
  802.7 5.2 copy-start.9
  804.6 3.3 copy-start.3
  975.7 3.9 copy-start.14
  978.5 1.1 copy-start.5
  984.9 1.0 copy-start.38
  986.8 262.0 %all-gather.13.cloned.1.call-start = ((), (), s32[]{:S(2)}) async-start(), calls=%async_computation.10 | async-start | bytes 2359296 | tf_op jit(solution)/shard_map/all_gather | solution.py:97
  986.8 2.5 copy-start.45
  989.3 1.9 copy-start.44
  989.3 1.9 copy-start.52
  991.3 1.9 copy-start.35
  994.4 4.6 copy-start.50
  1000.7 3.6 copy-start.10
  1002.0 2.3 copy-start.24
  1005.1 1.0 copy-start.27
  1006.0 160.6 %copy-start.4 = (f32[4,4,128,128]{3,2,1,0:T(8,128)S(1)}, f32[4,4,128,128]{3,2,1,0:T(8,128)}, u32[]{:S(2)}) copy-start(f32[4,4,128,128]{3,2,1,0:T(8,128)} %copy-done.2) | copy-start | bytes 3145732
  1166.6 1.9 copy-start.8
  1168.5 1.9 copy-start.1
  1170.5 2.3 copy-start.19
  1176.4 1.9 copy-start.41
  1176.4 1.9 copy-start.55
  1178.3 1.9 copy-start.36
  1200.1 5.0 copy-start.32
  1200.9 4.3 copy-start.6
  1200.9 4.3 copy-start.48
  1207.0 1.7 copy-start.30
  1211.0 44.2 %all-to-all-start.3 = ((bf16[4,512,128]{2,0,1:T(4,128)(2,1)}), bf16[4,512,128]{2,0,1:T(4,128)(2,1)}, u32[]{:S(2)}, u32[]{:S(2)}) async-start(bf16[4,512,128]{2,0,1:T(4,128)(2,1)} %copy.217), calls=%async_computation.3 | async-start | bytes 1048576 | tf_op jit(solution)/shard_map/all_to_all | solution.py:119
  1217.2 3.2 copy-start.16
  1225.6 4.1 copy-start.11
  1225.6 4.1 copy-start.25
  1232.6 20.3 %copy-start.34 = (f32[4,3,128,128]{2,3,1,0:T(8,128)S(1)}, f32[4,3,128,128]{2,3,1,0:T(8,128)}, u32[]{:S(2)}) copy-start(f32[4,3,128,128]{2,3,1,0:T(8,128)} %slice.45) | copy-start | bytes 2359300
  1248.8 4.8 copy-start.15
  1248.8 4.8 copy-start.23
  1253.6 5.7 copy-start.33
  1255.1 13.1 %all-to-all-start.5 = ((bf16[4,512,128]{2,0,1:T(4,128)(2,1)}), bf16[4,512,128]{2,0,1:T(4,128)(2,1)}, u32[]{:S(2)}, u32[]{:S(2)}) async-start(bf16[4,512,128]{2,0,1:T(4,128)(2,1)} %copy.230), calls=%async_computation.5 | async-start | bytes 1048576 | tf_op jit(solution)/shard_map/all_to_all | solution.py:120
  1259.3 1.1 copy-start.49
  1267.6 6.6 copy-start.28
  1268.2 12.3 all-to-all-start.7
  1271.7 2.5 copy-start.42
  1271.7 2.5 copy-start.46
  1280.5 12.3 all-to-all-start.6
  (3 other events, 2.9 us)
Sparse Core Ops, SparseCore 0:
  21.5 50.2 all-gather.8
  74.5 47.5 all-gather.10
  986.9 48.0 all-gather.14
  1201.0 47.7 all-gather.12
where the time goes:
time: 1300 us
  other arithmetic  1030 us (79%)
  matrix products  115 us (9%)
  local copies, waits for them, and re-layouts  50.9 us (4%)
  waiting for transfers between devices  46.2 us (4%)
  starting transfers between devices  26.1 us (2%)
  between operations  15 us (1%)
  blocking collectives  13.1 us (1%)
    another operation x6, other arithmetic, group_output(): low_gram = jnp.linalg.cholesky(gram_in)  350 us
    another operation x5, other arithmetic, group_output(): low_mix = jnp.linalg.cholesky(inner_mat + eye_rows)  349 us
    another operation x1, other arithmetic, group_output(): lax.linalg.triangular_solve(low_mix, first_pass, left_side=True, lower=Tr...  158 us
    another operation x2, other arithmetic, group_output(): lax.linalg.triangular_solve(low_gram, half_inv, left_side=True, lower=Tru...  158 us
    dot_general x31, matrix products, exact_einsum(): return jnp.einsum(form, left, right, precision=lax.Precision.HIGHEST)  69.1 us
  transfers between devices with their start and end apart: 11, of which 7 were waited for; matrix products, arithmetic and copies ran while one was open for 50% of the time, Pallas kernels for 0%

commit v1 on v0

v1 whole, which is shorter than its diff:
```python
import functools

import jax
import jax.numpy as jnp
from jax import lax
from jax.experimental import pallas as pl
from jax.experimental.pallas import tpu as pltpu
from jax.sharding import PartitionSpec as P

GROUP = 128
BASE = 32
VMEM_LIMIT = 56 * 1024 * 1024
F32 = jnp.float32
BF16 = jnp.bfloat16
DIMS = {
    "nn": (((1,), (0,)), ((), ())),
    "nt": (((1,), (1,)), ((), ())),
    "tn": (((0,), (0,)), ((), ())),
}


def parts(x, count):
    if isinstance(x, list):
        return x[:count]
    if x.dtype == BF16:
        return [x]
    found = []
    for i in range(count):
        term = x.astype(BF16)
        found.append(term)
        if i + 1 < count:
            x = x - term.astype(F32)
    return found


def mm(a, b, form="nn", count=2):
    left, right = parts(a, count), parts(b, count)
    total = None
    for i in reversed(range(len(left))):
        for j in reversed(range(len(right))):
            if i + j < count:
                term = lax.dot_general(left[i], right[j], DIMS[form], preferred_element_type=F32)
                total = term if total is None else total + term
    return total


def iota(shape, dim):
    return lax.broadcasted_iota(jnp.int32, shape, dim)


def take_block(ref, per_block, heads, head, block):
    rows = [ref[(block * per_block + r) * heads + head] for r in range(per_block)]
    return rows[0] if per_block == 1 else jnp.concatenate(rows, axis=0)


def put_block(ref, per_block, heads, head, block, value):
    size = value.shape[0] // per_block
    for r in range(per_block):
        ref[(block * per_block + r) * heads + head] = value[r * size : (r + 1) * size]


def eliminate(x, groups):
    shape = (groups, BASE, 128)
    flat = (groups * BASE, 128)
    lane = iota(shape, 2) % BASE
    row = iota(shape, 1)
    group_start = (iota(flat, 1) // BASE) * BASE
    x = x.reshape(shape)
    pivots = jnp.ones(shape, F32)
    for p in range(BASE):
        column = jnp.take_along_axis(
            x.reshape(flat), group_start + p, axis=1, mode="promise_in_bounds"
        ).reshape(shape)
        pivot = column[:, p : p + 1, :]
        pivots = jnp.where(row == p, pivot, pivots)
        if p + 1 < BASE:
            pivot_row = jnp.where(lane[:, p : p + 1] == p, 1.0, x[:, p : p + 1, :])
            scaled = pivot_row * (1.0 / pivot)
            keep = jnp.where(lane == p, 0.0, x)
            x = jnp.where(row > p, keep - column * scaled, x)
    unit = jnp.where(lane < row, x, jnp.where(lane == row, 1.0, 0.0))
    return (unit * lax.rsqrt(pivots)).reshape(flat)


def factor(a_ref, packed_ref, pairs, invert):
    groups = pairs // 4
    slab = (BASE, 128)
    square = (128, 128)

    def one_block(kb, carry):
        start = pl.multiple_of(kb * BASE, BASE)
        slab_group = iota(slab, 1) // BASE
        slabs = []
        for g in range(groups):
            joined = jnp.zeros(slab, F32)
            for h in range(4):
                rows = a_ref[4 * g + h, pl.ds(start, BASE), :]
                rows = pltpu.roll(rows, lax.rem((h - kb) * BASE + 128, 128), 1)
                joined = jnp.where(slab_group == h, rows, joined)
            slabs.append(joined)
        packed_ref[...] = eliminate(jnp.concatenate(slabs, axis=0), groups)

        def update(g, carry):
            packed = packed_ref[pl.ds(pl.multiple_of(g * BASE, BASE), BASE), :]
            row_block = iota(square, 0) // BASE
            col_block = iota(square, 1) // BASE
            eye = (iota(square, 0) == iota(square, 1)).astype(F32)
            for h in range(4):
                pair = 4 * g + h
                turned = pltpu.roll(packed, lax.rem((kb - h) * BASE + 128, 128), 1)
                low = parts(jnp.where(slab_group == kb, turned, 0.0), 3)
                a = a_ref[pair]
                with_eye = jnp.where((row_block == kb) & (col_block == kb), eye, a)
                top = mm(low, with_eye, "nn", 3)
                wide = mm(low, top, "tn", 3)
                new = jnp.where(col_block == kb, 0.0, a) - mm(a, wide, "nn", 3)
                if invert:
                    a_ref[pair] = jnp.where(row_block == kb, wide, new)
                else:
                    a_ref[pair] = jnp.where(row_block > kb, new, a)
                    a_ref[pair, pl.ds(start, BASE), :] = jnp.where(slab_group <= kb, top, 0.0)
            return carry

        lax.fori_loop(0, groups, update, 0)
        return carry

    lax.fori_loop(0, 128 // BASE, one_block, 0)


def sums_kernel(heads, blocks, per_block, k_ref, v_ref, out_ref):
    def one(head, carry):
        gram = jnp.zeros((128, 128), F32)
        state = jnp.zeros((128, 128), F32)
        for block in range(blocks):
            k = take_block(k_ref, per_block, heads, head, block)
            v = take_block(v_ref, per_block, heads, head, block)
            gram += mm(k, k, "tn")
            state += mm(v, k, "tn")
        out_ref[head] = gram
        out_ref[heads + head] = state
        return carry

    lax.fori_loop(0, heads, one, 0)


def main_kernel(
    heads, blocks, per_block,
    q_ref, k_ref, v_ref, g_ref, every_ref, regular_ref,
    o_ref, dq_ref, dk_ref, dv_ref, later_ref, sums_ref,
    p_ref, kp_ref, m_ref, state_ref, packed_ref,
):
    pairs = heads * blocks
    square = (128, 128)
    rank = lax.axis_index("seq")

    def prefix(head, carry):
        def add(s, so_far):
            return (so_far[0] + every_ref[s, head], so_far[1] + every_ref[s, heads + head])

        zero = jnp.zeros(square, F32)
        gram, state = lax.fori_loop(0, rank, add, (zero, zero))
        eye = iota(square, 0) == iota(square, 1)
        gram = gram + jnp.where(eye, regular_ref[pl.ds(head, 1), :], 0.0)
        for block in range(blocks):
            p_ref[head * blocks + block] = gram
            state_ref[head * blocks + block] = state
            if block + 1 < blocks:
                k = take_block(k_ref, per_block, heads, head, block)
                v = take_block(v_ref, per_block, heads, head, block)
                gram += mm(k, k, "tn")
                state += mm(v, k, "tn")
        return carry

    lax.fori_loop(0, heads, prefix, 0)
    factor(p_ref, packed_ref, pairs, True)

    def inner(head, carry):
        eye = (iota(square, 0) == iota(square, 1)).astype(F32)
        for block in range(blocks):
            pair = head * blocks + block
            k = take_block(k_ref, per_block, heads, head, block)
            kp = mm(k, p_ref[pair], "nn", 3)
            kp_ref[pair] = kp
            m_ref[pair] = eye + mm(kp, k, "nt", 3)
        return carry

    lax.fori_loop(0, heads, inner, 0)
    factor(m_ref, packed_ref, pairs, False)

    def outer(head, carry):
        upto = iota(square, 1) <= iota(square, 0)
        later_gram = jnp.zeros(square, F32)
        later_state = jnp.zeros(square, F32)
        for block in reversed(range(blocks)):
            pair = head * blocks + block
            q = take_block(q_ref, per_block, heads, head, block)
            k = take_block(k_ref, per_block, heads, head, block)
            v = take_block(v_ref, per_block, heads, head, block)
            g = take_block(g_ref, per_block, heads, head, block)
            inverse = parts(p_ref[pair], 3)
            kp = parts(kp_ref[pair], 3)
            m = parts(m_ref[pair], 3)
            state = parts(state_ref[pair], 2)

            def solve(rows):
                rows = parts(rows, 3)
                y = jnp.where(upto, mm(mm(rows, kp, "nt", 3), m, "nt", 3), 0.0)
                x = jnp.where(upto, mm(y, m, "nn", 3), 0.0)
                return mm(rows, inverse, "nn", 3) - mm(x, kp, "nn", 3)

            u = solve(q)
            ct = jnp.where(upto, mm(g, v, "nt"), 0.0)
            z = solve(mm(g, state, "nn") + mm(ct, k, "nn"))
            up, zp = parts(u, 2), parts(z, 2)
            wt = parts(jnp.where(upto, mm(up, k, "nt"), 0.0), 2)
            w2t = jnp.where(upto, mm(zp, k, "nt"), 0.0)
            put_block(o_ref, per_block, heads, head, block, (mm(up, state, "nt") + mm(wt, v, "nn")).astype(BF16))
            put_block(dq_ref, per_block, heads, head, block, z.astype(BF16))
            dk_ref[pair] = mm(ct - w2t, up, "tn") - mm(wt, zp, "tn")
            dv_ref[pair] = mm(wt, g, "tn")
            later_ref[pair] = later_gram
            later_ref[pairs + pair] = later_state
            zu = mm(zp, up, "tn")
            later_gram = later_gram - (zu + zu.T)
            later_state = later_state + mm(g, up, "tn")
        sums_ref[head] = later_gram
        sums_ref[heads + head] = later_state
        return carry

    lax.fori_loop(0, heads, outer, 0)


def last_kernel(
    heads, blocks, per_block, shards,
    k_ref, v_ref, dk_ref, dv_ref, later_ref, every_ref, dk_out, dv_out,
):
    pairs = heads * blocks
    rank = lax.axis_index("seq")

    def one(head, carry):
        def add(s, so_far):
            return (so_far[0] + every_ref[s, head], so_far[1] + every_ref[s, heads + head])

        zero = jnp.zeros((128, 128), F32)
        gram, state = lax.fori_loop(rank + 1, shards, add, (zero, zero))
        for block in range(blocks):
            pair = head * blocks + block
            k = take_block(k_ref, per_block, heads, head, block)
            v = take_block(v_ref, per_block, heads, head, block)
            sym = later_ref[pair] + gram
            after = parts(later_ref[pairs + pair] + state, 2)
            dk = dk_ref[pair] + mm(k, sym, "nn") + mm(v, after, "nn")
            dv = dv_ref[pair] + mm(k, after, "nt")
            put_block(dk_out, per_block, heads, head, block, dk.astype(BF16))
            put_block(dv_out, per_block, heads, head, block, dv.astype(BF16))
        return carry

    lax.fori_loop(0, heads, one, 0)


def call(body, inputs, out_shape, scratch=(), flops=10**9):
    vmem = pl.BlockSpec(memory_space=pltpu.VMEM)
    return pl.pallas_call(
        body,
        out_shape=out_shape,
        in_specs=[vmem] * len(inputs),
        out_specs=jax.tree.map(lambda _: vmem, out_shape),
        scratch_shapes=list(scratch),
        compiler_params=pltpu.CompilerParams(vmem_limit_bytes=VMEM_LIMIT),
        cost_estimate=pl.CostEstimate(flops=flops, bytes_accessed=8 * 2**20, transcendentals=0),
    )(*inputs)


def on_device(head_parts, seq_parts, queries, keys, values, out_grad, regular):
    local = queries.shape[1]
    feature = queries.shape[2]
    heads = queries.shape[0] // head_parts
    blocks = head_parts * local // GROUP
    per_block = GROUP // local
    pairs = heads * blocks

    def swap(x):
        return lax.all_to_all(x, "head", split_axis=0, concat_axis=0, tiled=True)

    keys, values = swap(keys), swap(values)
    queries, out_grad = swap(queries), swap(out_grad)
    square = (feature, feature)

    def shape(count, kind=F32, rows=feature):
        return jax.ShapeDtypeStruct((count, rows, feature), kind)

    moved = jax.ShapeDtypeStruct(queries.shape, BF16)
    sums = call(functools.partial(sums_kernel, heads, blocks, per_block), (keys, values), shape(2 * heads))
    every = lax.all_gather(sums, "seq", axis=0)
    output, dq, dk, dv, later, back = call(
        functools.partial(main_kernel, heads, blocks, per_block),
        (queries, keys, values, out_grad, every, regular),
        (moved, moved, shape(pairs), shape(pairs), shape(2 * pairs), shape(2 * heads)),
        [pltpu.VMEM((pairs,) + square, F32)] * 4 + [pltpu.VMEM((pairs // 4 * BASE, 128), F32)],
    )
    every_back = lax.all_gather(back, "seq", axis=0)
    output, dq = swap(output), swap(dq)
    dk, dv = call(
        functools.partial(last_kernel, heads, blocks, per_block, seq_parts),
        (keys, values, dk, dv, later, every_back),
        (moved, moved),
    )
    return output, dq, swap(dk), swap(dv)


def solution(mesh):
    placed = P(None, ("seq", "head"), None)
    return jax.shard_map(
        functools.partial(on_device, mesh.shape["head"], mesh.shape["seq"]),
        mesh=mesh,
        in_specs=(placed,) * 4 + (P("head", None),),
        out_specs=(placed,) * 4,
        check_vma=False,
    )
```

time: 1300 us -> 364 us (0.28)
  other arithmetic: 1030 us -> 0 us
  Pallas kernels: 0 us -> 148 us
  matrix products: 115 us -> 0 us
  blocking collectives: 13.1 us -> 87.6 us
  waiting for transfers between devices: 46.2 us -> 107 us
  local copies, waits for them, and re-layouts: 50.9 us -> 3.18 us
  starting transfers between devices: 26.1 us -> 3.55 us
    another operation x18 -> x0, other arithmetic: 1020 us -> none  [the longest x6 350 us: group_output(): low_gram = jnp.linalg.cholesky(gram_in)]
    pallas_call x0 -> x3, Pallas kernels: none -> 148 us  [call(): pl.pallas_call(body, out_shape=out_shape, in_specs=[vmem] * len(inputs),...]
    dot_general x39 -> x0, matrix products: 86.2 us -> none  [the longest x31 69.1 us: exact_einsum(): return jnp.einsum(form, left, right, precision=lax.Precision.HIGHEST)]
    all_gather x4 -> x2, waiting for transfers between devices: 30.9 us -> 107 us  [the longest x1 56.3 us: on_device(): every_back = lax.all_gather(back, 'seq', axis=0)]
    all_to_all x1 -> x7, blocking collectives: 13.1 us -> 87.6 us  [swap(): return lax.all_to_all(x, 'head', split_axis=0, concat_axis=0, tiled=True)]
    another operation x15 -> x0, matrix products: 29 us -> none  [the longest x3 7.71 us: group_output(): lax.linalg.triangular_solve(low_mix, right_side, left_side=True, lower=True)]
    all_to_all x7 -> x1, starting transfers between devices: 25.7 us -> 3.47 us  [swap(): return lax.all_to_all(x, 'head', split_axis=0, concat_axis=0, tiled=True)]
    all_to_all x7 -> x1, waiting for transfers between devices: 15.2 us -> 0.01 us  [swap(): return lax.all_to_all(x, 'head', split_axis=0, concat_axis=0, tiled=True)]
  transfers between devices with their start and end apart: 11 -> 3, of which waited for: 7 -> 2; matrix products, arithmetic and copies ran while one was open for 50% -> 0% of each run, Pallas kernels for 0% -> 2%
where the time goes in v1:
time: 364 us; the launch traced here: 363 us
  Pallas kernels  148 us (41%)
  waiting for transfers between devices  107 us (29%)
  blocking collectives  87.6 us (24%)
  between operations  14.1 us (4%)
    pallas_call x3, Pallas kernels, call(): pl.pallas_call(body, out_shape=out_shape, in_specs=[vmem] * len(inputs),...  148 us
    all_to_all x7, blocking collectives, swap(): return lax.all_to_all(x, 'head', split_axis=0, concat_axis=0, tiled=True)  87.6 us
    all_gather x1, waiting for transfers between devices, on_device(): every_back = lax.all_gather(back, 'seq', axis=0)  56.3 us
    all_gather x1, waiting for transfers between devices, on_device(): every = lax.all_gather(sums, 'seq', axis=0)  50.7 us
  transfers between devices with their start and end apart: 3, of which 2 were waited for; matrix products, arithmetic and copies ran while one was open for 0% of the time, Pallas kernels for 2%

profile of v1, /device:TPU:0, one launch (start us, length us, event | category | flops | bytes accessed | tf_op | source)
XLA Modules:
  0.0 363.2 jit_solution(2058169989129235522)
XLA Ops:
  7.2 0.0 copy-start
  7.2 0.0 copy-start.1
  7.2 0.0 all-gather.5.cloned.1.call-start
  7.2 13.8 %all_to_all.40.k_ref = bf16[16,128,128]{2,1,0:T(8,128)(2,1)} all-to-all(bf16[16,128,128]{2,1,0:T(8,128)(2,1)} %param.6), channel_id=1, replica_groups=mesh['seq'=8,'head'=4] {'head'}, dimensions={0} | all-to-all | bytes 1048576 | tf_op jit(solution)/shard_map/all_to_all | solution.py:283
  21.1 13.0 %all_to_all.41.v_ref = bf16[16,128,128]{2,1,0:T(8,128)(2,1)} all-to-all(bf16[16,128,128]{2,1,0:T(8,128)(2,1)} %param.7), channel_id=1, replica_groups=mesh['seq'=8,'head'=4] {'head'}, dimensions={0} | all-to-all | bytes 1048576 | tf_op jit(solution)/shard_map/all_to_all | solution.py:283
  34.1 3.0 shard_map.84
  37.1 0.0 all-gather.5.cloned.1.call-update
  37.2 0.0 all-gather.7.cloned.1.call-start
  37.2 0.0 copy-done
  37.2 11.9 %all_to_all.42.q_ref = bf16[16,128,128]{2,1,0:T(8,128)(2,1)} all-to-all(bf16[16,128,128]{2,1,0:T(8,128)(2,1)S(1)} %copy-done), channel_id=1, replica_groups=mesh['seq'=8,'head'=4] {'head'}, dimensions={0} | all-to-all | bytes 1048576 | tf_op jit(solution)/shard_map/all_to_all | solution.py:283
  49.2 0.0 copy-done.1
  49.2 11.9 %all_to_all.43.g_ref = bf16[16,128,128]{2,1,0:T(8,128)(2,1)} all-to-all(bf16[16,128,128]{2,1,0:T(8,128)(2,1)S(1)} %copy-done.1), channel_id=1, replica_groups=mesh['seq'=8,'head'=4] {'head'}, dimensions={0} | all-to-all | bytes 1048576 | tf_op jit(solution)/shard_map/all_to_all | solution.py:283
  61.1 50.7 %all-gather.5.cloned.1.call-done = f32[64,128,128]{2,1,0:T(8,128)} async-done(((f32[8,128,128]{2,1,0:T(8,128)}), f32[64,128,128]{2,1,0:T(8,128)}) %all-gather.5.cloned.1.call-update) | async-done | bytes 4194320 | tf_op jit(solution)/shard_map/all_gather | solution.py:294
  111.8 137.8 %shard_map.85 = (bf16[16,128,128]{2,1,0:T(8,128)(2,1)}, bf16[16,128,128]{2,1,0:T(8,128)(2,1)}, f32[16,128,128]{2,1,0:T(8,128)}, f32[16,128,128]{2,1,0:T(8,128)},...) custom-call(bf16[16,128,128]{2,1,0:T(8,128)(2,1)} %all_to_all.42.q_ref, bf16[16,128,128]{2,1,0:T(8,128)(2,1)} %all_to_all.40.k_ref, ...), custom_call_target="tpu_custom_call" | custom-call | flops 1000000000 | bytes 8388608 | tf_op jit(solution)/shard_map/pallas_call | solution.py:263
  249.6 0.0 all-gather.7.cloned.1.call-update
  249.6 12.3 %all_to_all.44 = bf16[16,128,128]{2,1,0:T(8,128)(2,1)S(1)} all-to-all(bf16[16,128,128]{2,1,0:T(8,128)(2,1)} %get-tuple-element.12), channel_id=1, replica_groups=mesh['seq'=8,'head'=4] {'head'}, dimensions={0} | all-to-all | bytes 1048576 | tf_op jit(solution)/shard_map/all_to_all | solution.py:283
  261.9 3.5 all-to-all-start.5
  265.4 56.3 %all-gather.7.cloned.1.call-done = f32[64,128,128]{2,1,0:T(8,128)} async-done(((f32[8,128,128]{2,1,0:T(8,128)}), f32[64,128,128]{2,1,0:T(8,128)}) %all-gather.7.cloned.1.call-update) | async-done | bytes 4194320 | tf_op jit(solution)/shard_map/all_gather | solution.py:301
  321.7 6.9 %shard_map.86 = (bf16[16,128,128]{2,1,0:T(8,128)(2,1)}, bf16[16,128,128]{2,1,0:T(8,128)(2,1)}) custom-call(bf16[16,128,128]{2,1,0:T(8,128)(2,1)} %all_to_all.40.k_ref, bf16[16,128,128]{2,1,0:T(8,128)(2,1)} %all_to_all.41.v_ref, f32[16,128,128]{2,1,0:T(8,128)} %get-tuple-element.14.dk_ref, f32[16,128,128]{2,1,0:T(8,128)} %get-tuple-element.15.dv_ref, ...), custom_call_target="tpu_custom_call" | custom-call | flops 1000000000 | bytes 8388608 | tf_op jit(solution)/shard_map/pallas_call | solution.py:263
  328.6 0.0 all-to-all-done.5
  328.6 12.3 %all_to_all.45 = bf16[16,128,128]{2,1,0:T(8,128)(2,1)S(1)} all-to-all(bf16[16,128,128]{2,1,0:T(8,128)(2,1)} %get-tuple-element.18), channel_id=1, replica_groups=mesh['seq'=8,'head'=4] {'head'}, dimensions={0} | all-to-all | bytes 1048576 | tf_op jit(solution)/shard_map/all_to_all | solution.py:283
  340.9 12.3 %all_to_all.46 = bf16[16,128,128]{2,1,0:T(8,128)(2,1)S(1)} all-to-all(bf16[16,128,128]{2,1,0:T(8,128)(2,1)} %get-tuple-element.19), channel_id=1, replica_groups=mesh['seq'=8,'head'=4] {'head'}, dimensions={0} | all-to-all | bytes 1048576 | tf_op jit(solution)/shard_map/all_to_all | solution.py:283
  353.2 0.8 copy.13
  354.0 0.8 copy.14
  354.8 0.8 copy.15
  355.6 0.8 copy.16
Async XLA Ops:
  7.2 30.1 %copy-start = (bf16[16,128,128]{2,1,0:T(8,128)(2,1)S(1)}, bf16[16,128,128]{2,1,0:T(8,128)(2,1)}, u32[]{:S(2)}) copy-start(bf16[16,128,128]{2,1,0:T(8,128)(2,1)} %param.5) | copy-start | bytes 1572868
  7.2 42.0 %copy-start.1 = (bf16[16,128,128]{2,1,0:T(8,128)(2,1)S(1)}, bf16[16,128,128]{2,1,0:T(8,128)(2,1)}, u32[]{:S(2)}) copy-start(bf16[16,128,128]{2,1,0:T(8,128)(2,1)} %param.8) | copy-start | bytes 1572868
  7.2 104.6 %all-gather.5.cloned.1.call-start = ((), (), s32[]{:S(2)}) async-start(), calls=%async_computation.8 | async-start | bytes 4718592 | tf_op jit(solution)/shard_map/all_gather | solution.py:294
  37.2 284.6 %all-gather.7.cloned.1.call-start = ((), (), s32[]{:S(2)}) async-start(), calls=%async_computation.9 | async-start | bytes 4718592 | tf_op jit(solution)/shard_map/all_gather | solution.py:301
  261.9 66.7 %all-to-all-start.5 = ((bf16[16,128,128]{2,1,0:T(8,128)(2,1)}), bf16[16,128,128]{2,1,0:T(8,128)(2,1)S(1)}, u32[]{:S(2)}, u32[]{:S(2)}) async-start(bf16[16,128,128]{2,1,0:T(8,128)(2,1)} %get-tuple-element.13), calls=%async_computation.5 | async-start | bytes 1048576 | tf_op jit(solution)/shard_map/all_to_all | solution.py:283
Sparse Core Ops, SparseCore 0:
  37.3 74.4 all-gather.4
  249.7 71.9 all-gather.6

commit v2 on v1

--- a/solution.py
+++ b/solution.py
@@ -127,38 +127,195 @@
     lax.fori_loop(0, 128 // BASE, one_block, 0)
 
 
-def sums_kernel(heads, blocks, per_block, k_ref, v_ref, out_ref):
-    def one(head, carry):
+def group_size(shards):
+    size = 1
+    while 4 * size * size <= shards and shards % (2 * size) == 0:
+        size *= 2
+    return size
+
+
+def send(src, dst, send_sem, recv_sem, where):
+    return pltpu.make_async_remote_copy(
+        src_ref=src, dst_ref=dst, send_sem=send_sem, recv_sem=recv_sem,
+        device_id=where, device_id_type=pl.DeviceIdType.MESH,
+    )
+
+
+def meet(head_parts, shards):
+    size = group_size(shards)
+    rank, me = lax.axis_index("seq"), lax.axis_index("head")
+    outer, inner = rank // size, rank % size
+    barrier = pltpu.get_barrier_semaphore()
+
+    def greet(where):
+        pl.semaphore_signal(barrier, inc=1, device_id=where, device_id_type=pl.DeviceIdType.MESH)
+
+    for d in range(1, head_parts):
+        greet((rank, lax.rem(me + d, head_parts)))
+    for d in range(1, size):
+        greet((outer * size + lax.rem(inner + d, size), me))
+
+    @pl.when(outer > 0)
+    def _():
+        greet((rank - size, me))
+
+    @pl.when(outer < shards // size - 1)
+    def _():
+        greet((rank + size, me))
+
+    chained = jnp.where(outer > 0, 1, 0) + jnp.where(outer < shards // size - 1, 1, 0)
+    pl.semaphore_wait(barrier, head_parts - 1 + size - 1 + chained)
+
+
+class Scan:
+    def __init__(self, shards, backward, own, near, before, total, sems):
+        self.size = group_size(shards)
+        self.count = shards // self.size
+        self.rank, self.me = lax.axis_index("seq"), lax.axis_index("head")
+        self.step = -self.size if backward else self.size
+        self.base = self.rank // self.size * self.size
+        self.inner = self.rank % self.size
+        outer = self.rank // self.size
+        self.outer = self.count - 1 - outer if backward else outer
+        self.backward = backward
+        self.own, self.near, self.before, self.total = own, near, before, total
+        self.near_send, self.near_recv, self.far_send, self.far_recv = sems
+
+    def near_copy(self, c, d):
+        where = (self.base + lax.rem(self.inner + d, self.size), self.me)
+        return send(
+            self.own.at[c], self.near.at[d - 1, c],
+            self.near_send.at[d - 1, c], self.near_recv.at[d - 1, c], where,
+        )
+
+    def far_copy(self, c):
+        where = (self.rank + self.step, self.me)
+        return send(self.total.at[c], self.before.at[c], self.far_send.at[c], self.far_recv.at[c], where)
+
+    def start(self, c):
+        for d in range(1, self.size):
+            self.near_copy(c, d).start()
+
+    def finish(self, c):
+        whole = self.own[c]
+        lower = jnp.zeros(whole.shape, F32)
+        for d in range(1, self.size):
+            self.near_copy(c, d).wait_recv()
+            other = self.near[d - 1, c]
+            whole = whole + other
+            counts = d > self.inner if self.backward else d <= self.inner
+            lower = lower + jnp.where(counts, other, 0.0)
+
+        @pl.when(self.outer == 0)
+        def _():
+            self.before[c] = jnp.zeros(whole.shape, F32)
+
+        @pl.when(self.outer > 0)
+        def _():
+            self.far_copy(c).wait_recv()
+
+        before = self.before[c]
+
+        @pl.when(self.outer < self.count - 1)
+        def _():
+            self.total[c] = before + whole
+            self.far_copy(c).start()
+
+        return before + lower
+
+    def drain(self, c):
+        for d in range(1, self.size):
+            self.near_copy(c, d).wait_send()
+
+        @pl.when(self.outer < self.count - 1)
+        def _():
+            self.far_copy(c).wait_send()
+
+
+def scan_scratch(shards, heads, square):
+    size = group_size(shards)
+    count = 2 * heads
+    near = (max(size - 1, 1), count)
+    dma = pltpu.SemaphoreType.DMA
+    return [
+        pltpu.VMEM(near + square, F32), pltpu.VMEM((count,) + square, F32),
+        pltpu.VMEM((count,) + square, F32), dma(near), dma(near), dma((count,)), dma((count,)),
+    ]
+
+
+def first_kernel(
+    heads, blocks, per_block, head_parts, shards,
+    q_in, k_in, v_in, g_in, q_ref, k_ref, v_ref, g_ref, before_ref,
+    own, near, before, total, near_send, near_recv, far_send, far_recv,
+    one_send, one_recv, all_send, all_recv,
+):
+    rank, me = lax.axis_index("seq"), lax.axis_index("head")
+    meet(head_parts, shards)
+    scan = Scan(shards, False, own, near, before, total, (near_send, near_recv, far_send, far_recv))
+
+    def one_copy(i, d, h):
+        src, dst = ((k_in, k_ref), (v_in, v_ref))[i]
+        peer = lax.rem(me + d, head_parts)
+        return send(
+            src.at[peer * heads + h], dst.at[me * heads + h],
+            one_send.at[i, d - 1, h], one_recv.at[i, d - 1, h], (rank, peer),
+        )
+
+    def all_copy(i, d):
+        src, dst = ((q_in, q_ref), (g_in, g_ref))[i]
+        peer = lax.rem(me + d, head_parts)
+        return send(
+            src.at[pl.ds(peer * heads, heads)], dst.at[pl.ds(me * heads, heads)],
+            all_send.at[i, d - 1], all_recv.at[i, d - 1], (rank, peer),
+        )
+
+    steps = [(i, d, h) for h in range(heads) for i in range(2) for d in range(1, head_parts)]
+    wholes = [(i, d) for i in range(2) for d in range(1, head_parts)]
+    for step in steps:
+        one_copy(*step).start()
+    for step in wholes:
+        all_copy(*step).start()
+    for src, dst in ((k_in, k_ref), (v_in, v_ref), (q_in, q_ref), (g_in, g_ref)):
+        for h in range(heads):
+            dst[me * heads + h] = src[me * heads + h]
+    for h in range(heads):
+        for i in range(2):
+            for d in range(1, head_parts):
+                one_copy(i, d, h).wait_recv()
         gram = jnp.zeros((128, 128), F32)
         state = jnp.zeros((128, 128), F32)
         for block in range(blocks):
-            k = take_block(k_ref, per_block, heads, head, block)
-            v = take_block(v_ref, per_block, heads, head, block)
+            k = take_block(k_ref, per_block, heads, h, block)
+            v = take_block(v_ref, per_block, heads, h, block)
             gram += mm(k, k, "tn")
             state += mm(v, k, "tn")
-        out_ref[head] = gram
-        out_ref[heads + head] = state
-        return carry
-
-    lax.fori_loop(0, heads, one, 0)
+        own[2 * h] = gram
+        own[2 * h + 1] = state
+        scan.start(2 * h)
+        scan.start(2 * h + 1)
+    for c in range(2 * heads):
+        before_ref[c] = scan.finish(c)
+    for step in wholes:
+        all_copy(*step).wait_recv()
+    for c in range(2 * heads):
+        scan.drain(c)
+    for step in steps:
+        one_copy(*step).wait_send()
+    for step in wholes:
+        all_copy(*step).wait_send()
 
 
 def main_kernel(
     heads, blocks, per_block,
-    q_ref, k_ref, v_ref, g_ref, every_ref, regular_ref,
+    q_ref, k_ref, v_ref, g_ref, before_ref, regular_ref,
     o_ref, dq_ref, dk_ref, dv_ref, later_ref, sums_ref,
     p_ref, kp_ref, m_ref, state_ref, packed_ref,
 ):
     pairs = heads * blocks
     square = (128, 128)
-    rank = lax.axis_index("seq")
 
     def prefix(head, carry):
-        def add(s, so_far):
-            return (so_far[0] + every_ref[s, head], so_far[1] + every_ref[s, heads + head])
-
-        zero = jnp.zeros(square, F32)
-        gram, state = lax.fori_loop(0, rank, add, (zero, zero))
+        gram, state = before_ref[2 * head], before_ref[2 * head + 1]
         eye = iota(square, 0) == iota(square, 1)
         gram = gram + jnp.where(eye, regular_ref[pl.ds(head, 1), :], 0.0)
         for block in range(blocks):
@@ -223,42 +380,79 @@
             zu = mm(zp, up, "tn")
             later_gram = later_gram - (zu + zu.T)
             later_state = later_state + mm(g, up, "tn")
-        sums_ref[head] = later_gram
-        sums_ref[heads + head] = later_state
+        sums_ref[2 * head] = later_gram
+        sums_ref[2 * head + 1] = later_state
         return carry
 
     lax.fori_loop(0, heads, outer, 0)
 
 
 def last_kernel(
-    heads, blocks, per_block, shards,
-    k_ref, v_ref, dk_ref, dv_ref, later_ref, every_ref, dk_out, dv_out,
+    heads, blocks, per_block, head_parts, shards,
+    o_in, dq_in, k_ref, v_ref, dk_ref, dv_ref, later_ref, own, o_out, dq_out, dk_out, dv_out,
+    dk_all, dv_all, near, after, total, near_send, near_recv, far_send, far_recv,
+    one_send, one_recv, all_send, all_recv,
 ):
     pairs = heads * blocks
-    rank = lax.axis_index("seq")
-
-    def one(head, carry):
-        def add(s, so_far):
-            return (so_far[0] + every_ref[s, head], so_far[1] + every_ref[s, heads + head])
-
-        zero = jnp.zeros((128, 128), F32)
-        gram, state = lax.fori_loop(rank + 1, shards, add, (zero, zero))
+    rank, me = lax.axis_index("seq"), lax.axis_index("head")
+    meet(head_parts, shards)
+    scan = Scan(shards, True, own, near, after, total, (near_send, near_recv, far_send, far_recv))
+
+    def one_copy(i, d, h):
+        src, dst = ((dk_all, dk_out), (dv_all, dv_out))[i]
+        peer = lax.rem(me + d, head_parts)
+        return send(
+            src.at[peer * heads + h], dst.at[me * heads + h],
+            one_send.at[i, d - 1, h], one_recv.at[i, d - 1, h], (rank, peer),
+        )
+
+    def all_copy(i, d):
+        src, dst = ((o_in, o_out), (dq_in, dq_out))[i]
+        peer = lax.rem(me + d, head_parts)
+        return send(
+            src.at[pl.ds(peer * heads, heads)], dst.at[pl.ds(me * heads, heads)],
+            all_send.at[i, d - 1], all_recv.at[i, d - 1], (rank, peer),
+        )
+
+    steps = [(i, d, h) for h in range(heads) for i in range(2) for d in range(1, head_parts)]
+    wholes = [(i, d) for i in range(2) for d in range(1, head_parts)]
+    for c in range(2 * heads):
+        scan.start(c)
+    for step in wholes:
+        all_copy(*step).start()
+    for src, dst in ((o_in, o_out), (dq_in, dq_out)):
+        for h in range(heads):
+            dst[me * heads + h] = src[me * heads + h]
+    for h in range(heads):
+        gram, state = scan.finish(2 * h), scan.finish(2 * h + 1)
         for block in range(blocks):
-            pair = head * blocks + block
-            k = take_block(k_ref, per_block, heads, head, block)
-            v = take_block(v_ref, per_block, heads, head, block)
+            pair = h * blocks + block
+            k = take_block(k_ref, per_block, heads, h, block)
+            v = take_block(v_ref, per_block, heads, h, block)
             sym = later_ref[pair] + gram
-            after = parts(later_ref[pairs + pair] + state, 2)
-            dk = dk_ref[pair] + mm(k, sym, "nn") + mm(v, after, "nn")
-            dv = dv_ref[pair] + mm(k, after, "nt")
-            put_block(dk_out, per_block, heads, head, block, dk.astype(BF16))
-            put_block(dv_out, per_block, heads, head, block, dv.astype(BF16))
-        return carry
-
-    lax.fori_loop(0, heads, one, 0)
-
-
-def call(body, inputs, out_shape, scratch=(), flops=10**9):
+            state_after = parts(later_ref[pairs + pair] + state, 2)
+            dk = dk_ref[pair] + mm(k, sym, "nn") + mm(v, state_after, "nn")
+            dv = dv_ref[pair] + mm(k, state_after, "nt")
+            put_block(dk_all, per_block, heads, h, block, dk.astype(BF16))
+            put_block(dv_all, per_block, heads, h, block, dv.astype(BF16))
+        for i in range(2):
+            for d in range(1, head_parts):
+                one_copy(i, d, h).start()
+        dk_out[me * heads + h] = dk_all[me * heads + h]
+        dv_out[me * heads + h] = dv_all[me * heads + h]
+    for step in wholes:
+        all_copy(*step).wait_recv()
+    for step in steps:
+        one_copy(*step).wait_recv()
+    for c in range(2 * heads):
+        scan.drain(c)
+    for step in wholes:
+        all_copy(*step).wait_send()
+    for step in steps:
+        one_copy(*step).wait_send()
+
+
+def call(body, inputs, out_shape, scratch=(), flops=10**9, **params):
     vmem = pl.BlockSpec(memory_space=pltpu.VMEM)
     return pl.pallas_call(
         body,
@@ -266,7 +460,7 @@
         in_specs=[vmem] * len(inputs),
         out_specs=jax.tree.map(lambda _: vmem, out_shape),
         scratch_shapes=list(scratch),
-        compiler_params=pltpu.CompilerParams(vmem_limit_bytes=VMEM_LIMIT),
+        compiler_params=pltpu.CompilerParams(vmem_limit_bytes=VMEM_LIMIT, **params),
         cost_estimate=pl.CostEstimate(flops=flops, bytes_accessed=8 * 2**20, transcendentals=0),
     )(*inputs)
 
@@ -279,33 +473,37 @@
     per_block = GROUP // local
     pairs = heads * blocks
 
-    def swap(x):
-        return lax.all_to_all(x, "head", split_axis=0, concat_axis=0, tiled=True)
-
-    keys, values = swap(keys), swap(values)
-    queries, out_grad = swap(queries), swap(out_grad)
     square = (feature, feature)
 
     def shape(count, kind=F32, rows=feature):
         return jax.ShapeDtypeStruct((count, rows, feature), kind)
 
     moved = jax.ShapeDtypeStruct(queries.shape, BF16)
-    sums = call(functools.partial(sums_kernel, heads, blocks, per_block), (keys, values), shape(2 * heads))
-    every = lax.all_gather(sums, "seq", axis=0)
+    square_sums = shape(2 * heads)
+    dma = pltpu.SemaphoreType.DMA
+    away = max(head_parts - 1, 1)
+    swap_sems = [dma((2, away, heads))] * 2 + [dma((2, away))] * 2
+    sizes = (heads, blocks, per_block)
+    queries, keys, values, out_grad, before = call(
+        functools.partial(first_kernel, *sizes, head_parts, seq_parts),
+        (queries, keys, values, out_grad),
+        (moved,) * 4 + (square_sums,),
+        [pltpu.VMEM((2 * heads,) + square, F32)] + scan_scratch(seq_parts, heads, square) + swap_sems,
+        collective_id=0, has_side_effects=True,
+    )
     output, dq, dk, dv, later, back = call(
-        functools.partial(main_kernel, heads, blocks, per_block),
-        (queries, keys, values, out_grad, every, regular),
-        (moved, moved, shape(pairs), shape(pairs), shape(2 * pairs), shape(2 * heads)),
+        functools.partial(main_kernel, *sizes),
+        (queries, keys, values, out_grad, before, regular),
+        (moved, moved, shape(pairs), shape(pairs), shape(2 * pairs), square_sums),
         [pltpu.VMEM((pairs,) + square, F32)] * 4 + [pltpu.VMEM((pairs // 4 * BASE, 128), F32)],
     )
-    every_back = lax.all_gather(back, "seq", axis=0)
-    output, dq = swap(output), swap(dq)
-    dk, dv = call(
-        functools.partial(last_kernel, heads, blocks, per_block, seq_parts),
-        (keys, values, dk, dv, later, every_back),
-        (moved, moved),
+    return call(
+        functools.partial(last_kernel, *sizes, head_parts, seq_parts),
+        (output, dq, keys, values, dk, dv, later, back),
+        (moved,) * 4,
+        [pltpu.VMEM(moved.shape, BF16)] * 2 + scan_scratch(seq_parts, heads, square) + swap_sems,
+        collective_id=1, has_side_effects=True,
     )
-    return output, dq, swap(dk), swap(dv)
 
 
 def solution(mesh):

time: 364 us -> 220 us (0.60)
  waiting for transfers between devices: 107 us -> 0 us
  blocking collectives: 87.6 us -> 0 us
  Pallas kernels: 148 us -> 213 us
  between operations: 14.1 us -> 0.67 us
    all_gather x2 -> x0, waiting for transfers between devices: 107 us -> none  [the longest x1 56.3 us: on_device(): every_back = lax.all_gather(back, 'seq', axis=0)]
    all_to_all x7 -> x0, blocking collectives: 87.6 us -> none  [swap(): return lax.all_to_all(x, 'head', split_axis=0, concat_axis=0, tiled=True)]
    pallas_call x3, Pallas kernels: 148 us -> 213 us  [call(): pl.pallas_call(body, out_shape=out_shape, in_specs=[vmem] * len(inputs),...]
  transfers between devices with their start and end apart: 3 -> 0, of which waited for: 2 -> 0; matrix products, arithmetic and copies ran while one was open for 0% -> 0% of each run, Pallas kernels for 2% -> 0%
where the time goes in v2:
time: 220 us; the launch traced here: 219 us
  Pallas kernels  213 us (97%)
  local copies, waits for them, and re-layouts  5.45 us (2%)
    pallas_call x3, Pallas kernels, call(): pl.pallas_call(body, out_shape=out_shape, in_specs=[vmem] * len(inputs),...  213 us
    unnamed x8, local copies, waits for them, and re-layouts  5.45 us

profile of v2, /device:TPU:0, one launch (start us, length us, event | category | flops | bytes accessed | tf_op | source)
XLA Modules:
  0.0 219.3 jit_solution(8941136345583985005)
XLA Ops:
  0.6 33.0 %shard_map.84 = (bf16[16,128,128]{2,1,0:T(8,128)(2,1)}, bf16[16,128,128]{2,1,0:T(8,128)(2,1)}, bf16[16,128,128]{2,1,0:T(8,128)(2,1)}, bf16[16,128,128]{2,1,0:T(8,128)(2,1)}, f32[8,128,128]{2,1,0:T(8,128)}) custom-call(bf16[16,128,128]{2,1,0:T(8,128)(2,1)} %q_in.1, bf16[16,128,128]{2,1,0:T(8,128)(2,1)} %k_in.1, bf16[16,128,128]{2,1,0:T(8,128)(2,1)} %v_in.1, ...), custom_call_target="tpu_custom_call" | custom-call | flops 1000000000 | bytes 8388608 | tf_op jit(solution)/shard_map/pallas_call | solution.py:457
  33.7 136.6 %shard_map.85 = (bf16[16,128,128]{2,1,0:T(8,128)(2,1)}, bf16[16,128,128]{2,1,0:T(8,128)(2,1)}, f32[16,128,128]{2,1,0:T(8,128)}, f32[16,128,128]{2,1,0:T(8,128)},...) custom-call(bf16[16,128,128]{2,1,0:T(8,128)(2,1)} %get-tuple-element.15.q_ref, ...), custom_call_target="tpu_custom_call" | custom-call | flops 1000000000 | bytes 8388608 | tf_op jit(solution)/shard_map/pallas_call | solution.py:457
  170.3 43.6 %shard_map.86 = (bf16[16,128,128]{2,1,0:T(8,128)(2,1)}, bf16[16,128,128]{2,1,0:T(8,128)(2,1)}, bf16[16,128,128]{2,1,0:T(8,128)(2,1)}, bf16[16,128,128]{2,1,0:T(8,128)(2,1)}) custom-call(bf16[16,128,128]{2,1,0:T(8,128)(2,1)} %get-tuple-element.20.o_in, bf16[16,128,128]{2,1,0:T(8,128)(2,1)} %get-tuple-element.21.dq_in, ...), custom_call_target="tpu_custom_call" | custom-call | flops 1000000000 | bytes 8388608 | tf_op jit(solution)/shard_map/pallas_call | solution.py:457
  213.9 0.0 copy-start.1
  213.9 0.0 copy-start
  213.9 2.0 copy.13
  215.9 1.9 copy.14
  217.7 0.0 copy-done.1
  217.7 0.8 copy.15
  218.5 0.0 copy-done
  218.5 0.8 copy.16
Async XLA Ops:
  213.9 3.9 %copy-start.1 = (bf16[16,128,128]{2,1,0:T(8,128)(2,1)S(1)}, bf16[16,128,128]{2,1,0:T(8,128)(2,1)}, u32[]{:S(2)}) copy-start(bf16[16,128,128]{2,1,0:T(8,128)(2,1)} %get-tuple-element.32) | copy-start | bytes 1572868
  213.9 4.7 %copy-start = (bf16[16,128,128]{2,1,0:T(8,128)(2,1)S(1)}, bf16[16,128,128]{2,1,0:T(8,128)(2,1)}, u32[]{:S(2)}) copy-start(bf16[16,128,128]{2,1,0:T(8,128)(2,1)} %get-tuple-element.33) | copy-start | bytes 1572868

commit v3 on v2

--- a/solution.py
+++ b/solution.py
@@ -35,13 +35,37 @@
 
 def mm(a, b, form="nn", count=2):
     left, right = parts(a, count), parts(b, count)
-    total = None
-    for i in reversed(range(len(left))):
-        for j in reversed(range(len(right))):
-            if i + j < count:
-                term = lax.dot_general(left[i], right[j], DIMS[form], preferred_element_type=F32)
-                total = term if total is None else total + term
-    return total
+    pairs = [(i, j) for i in range(len(left)) for j in range(len(right)) if i + j < count]
+    left = [left[i] for i, _ in pairs]
+    right = [right[j] for _, j in pairs]
+    if len(pairs) > 1:
+        left = jnp.concatenate(left, axis=0 if form == "tn" else 1)
+        right = jnp.concatenate(right, axis=1 if form == "nt" else 0)
+    else:
+        left, right = left[0], right[0]
+    return lax.dot_general(left, right, DIMS[form], preferred_element_type=F32)
+
+
+def spread(x, group, wanted):
+    x = jnp.where(group == wanted, x, 0.0)
+    x = x + pltpu.roll(x, BASE, 1)
+    return x + pltpu.roll(x, 2 * BASE, 1)
+
+
+def pack_left(x, group):
+    first = x.astype(BF16).astype(F32)
+    rest = x - first
+    second = rest.astype(BF16).astype(F32)
+    third = rest - second
+    one = jnp.where(group < 3, first, second)
+    two = jnp.where(group == 0, second, jnp.where(group == 1, third, 0.0))
+    return jnp.concatenate([one.astype(BF16), two.astype(BF16)], axis=1)
+
+
+def pack_right(y):
+    first, second, third = parts(y, 3)
+    none = jnp.zeros(y.shape, BF16)
+    return jnp.concatenate([first, second, third, first, second, first, none, none], axis=0)
 
 
 def iota(shape, dim):
@@ -60,26 +84,36 @@
 
 
 def eliminate(x, groups):
-    shape = (groups, BASE, 128)
-    flat = (groups * BASE, 128)
-    lane = iota(shape, 2) % BASE
-    row = iota(shape, 1)
+    tile = (groups, 8, 128)
+    flat = (groups * 8, 128)
+    lane = iota(tile, 2) % BASE
+    row = iota(tile, 1)
     group_start = (iota(flat, 1) // BASE) * BASE
-    x = x.reshape(shape)
-    pivots = jnp.ones(shape, F32)
-    for p in range(BASE):
-        column = jnp.take_along_axis(
-            x.reshape(flat), group_start + p, axis=1, mode="promise_in_bounds"
-        ).reshape(shape)
-        pivot = column[:, p : p + 1, :]
-        pivots = jnp.where(row == p, pivot, pivots)
-        if p + 1 < BASE:
-            pivot_row = jnp.where(lane[:, p : p + 1] == p, 1.0, x[:, p : p + 1, :])
-            scaled = pivot_row * (1.0 / pivot)
-            keep = jnp.where(lane == p, 0.0, x)
-            x = jnp.where(row > p, keep - column * scaled, x)
-    unit = jnp.where(lane < row, x, jnp.where(lane == row, 1.0, 0.0))
-    return (unit * lax.rsqrt(pivots)).reshape(flat)
+    x = x.reshape((groups, BASE, 128))
+    tiles = [x[:, 8 * t : 8 * t + 8, :] for t in range(BASE // 8)]
+
+    def pick(x, index):
+        return jnp.take_along_axis(
+            x.reshape(flat), index, axis=1, mode="promise_in_bounds"
+        ).reshape(tile)
+
+    for p in range(BASE - 1):
+        home, at = p // 8, p % 8
+        columns = {t: pick(tiles[t], group_start + p) for t in range(home, BASE // 8)}
+        pivot = columns[home][:, at : at + 1, :]
+        here = lane[:, :1] == p
+        pivot_row = jnp.where(here, 1.0, tiles[home][:, at : at + 1, :])
+        scaled = pivot_row * (1.0 / pivot)
+        for t in range((p + 1) // 8, BASE // 8):
+            new = jnp.where(lane == p, 0.0, tiles[t]) - columns[t] * scaled
+            tiles[t] = jnp.where(row > at, new, tiles[t]) if t == home else new
+    found = []
+    for t in range(BASE // 8):
+        pivots = pick(tiles[t], group_start + 8 * t + iota(flat, 0) % 8)
+        position = row + 8 * t
+        unit = jnp.where(lane < position, tiles[t], jnp.where(lane == position, 1.0, 0.0))
+        found.append(unit * lax.rsqrt(pivots))
+    return jnp.concatenate(found, axis=1).reshape(groups * BASE, 128)
 
 
 def factor(a_ref, packed_ref, pairs, invert):
@@ -102,20 +136,24 @@
 
         def update(g, carry):
             packed = packed_ref[pl.ds(pl.multiple_of(g * BASE, BASE), BASE), :]
+            turned = jnp.concatenate([packed, jnp.zeros((128 - BASE, 128), F32)], axis=0).T
             row_block = iota(square, 0) // BASE
             col_block = iota(square, 1) // BASE
-            eye = (iota(square, 0) == iota(square, 1)).astype(F32)
+            own = iota(slab, 1) == iota(slab, 0) + start
             for h in range(4):
                 pair = 4 * g + h
-                turned = pltpu.roll(packed, lax.rem((kb - h) * BASE + 128, 128), 1)
-                low = parts(jnp.where(slab_group == kb, turned, 0.0), 3)
+                low = pack_left(spread(packed, slab_group, h), slab_group)
+                low_t = pack_left(spread(turned[BASE * h : BASE * (h + 1)], slab_group, 0), slab_group)
                 a = a_ref[pair]
-                with_eye = jnp.where((row_block == kb) & (col_block == kb), eye, a)
-                top = mm(low, with_eye, "nn", 3)
-                wide = mm(low, top, "tn", 3)
-                new = jnp.where(col_block == kb, 0.0, a) - mm(a, wide, "nn", 3)
+                rows = a_ref[pair, pl.ds(start, BASE), :]
+                rows = jnp.where(slab_group == kb, jnp.where(own, 1.0, 0.0), rows)
+                top = mm(low, pack_right(rows))
+                wide = mm(low_t, pack_right(top))
+                gain = mm(pack_left(spread(a, col_block, kb), col_block), pack_right(wide))
+                new = jnp.where(col_block == kb, 0.0, a) - gain
                 if invert:
-                    a_ref[pair] = jnp.where(row_block == kb, wide, new)
+                    a_ref[pair] = new
+                    a_ref[pair, pl.ds(start, BASE), :] = wide
                 else:
                     a_ref[pair] = jnp.where(row_block > kb, new, a)
                     a_ref[pair, pl.ds(start, BASE), :] = jnp.where(slab_group <= kb, top, 0.0)
@@ -346,6 +384,7 @@
 
     def outer(head, carry):
         upto = iota(square, 1) <= iota(square, 0)
+        upto2 = iota((256, 128), 1) <= iota((256, 128), 0) % 128
         later_gram = jnp.zeros(square, F32)
         later_state = jnp.zeros(square, F32)
         for block in reversed(range(blocks)):
@@ -354,26 +393,27 @@
             k = take_block(k_ref, per_block, heads, head, block)
             v = take_block(v_ref, per_block, heads, head, block)
             g = take_block(g_ref, per_block, heads, head, block)
-            inverse = parts(p_ref[pair], 3)
             kp = parts(kp_ref[pair], 3)
             m = parts(m_ref[pair], 3)
             state = parts(state_ref[pair], 2)
-
-            def solve(rows):
-                rows = parts(rows, 3)
-                y = jnp.where(upto, mm(mm(rows, kp, "nt", 3), m, "nt", 3), 0.0)
-                x = jnp.where(upto, mm(y, m, "nn", 3), 0.0)
-                return mm(rows, inverse, "nn", 3) - mm(x, kp, "nn", 3)
-
-            u = solve(q)
+            both = [jnp.concatenate([p, r], axis=0) for p, r in zip(parts(p_ref[pair], 3), kp)]
             ct = jnp.where(upto, mm(g, v, "nt"), 0.0)
-            z = solve(mm(g, state, "nn") + mm(ct, k, "nn"))
-            up, zp = parts(u, 2), parts(z, 2)
-            wt = parts(jnp.where(upto, mm(up, k, "nt"), 0.0), 2)
-            w2t = jnp.where(upto, mm(zp, k, "nt"), 0.0)
+            rows = parts(mm(g, state, "nn") + mm(ct, k, "nn"), 3)
+            none = jnp.zeros(square, BF16)
+            rows = [jnp.concatenate([q if i == 0 else none, r], axis=0) for i, r in enumerate(rows)]
+            firsts = mm(rows, both, "nt", 3)
+            y = jnp.where(upto2, mm(firsts[:, 128:], m, "nt", 3), 0.0)
+            x = jnp.where(upto2, mm(y, m, "nn", 3), 0.0)
+            uz = firsts[:, :128] - mm(x, kp, "nn", 3)
+            u, z = uz[:128], uz[128:]
+            uzp = parts(uz, 2)
+            up, zp = [t[:128] for t in uzp], [t[128:] for t in uzp]
+            both_w = jnp.where(upto2, mm(uzp, k, "nt"), 0.0)
+            wt = parts(both_w[:128], 2)
+            w2t = both_w[128:]
             put_block(o_ref, per_block, heads, head, block, (mm(up, state, "nt") + mm(wt, v, "nn")).astype(BF16))
             put_block(dq_ref, per_block, heads, head, block, z.astype(BF16))
-            dk_ref[pair] = mm(ct - w2t, up, "tn") - mm(wt, zp, "tn")
+            dk_ref[pair] = mm(jnp.concatenate([ct - w2t, -both_w[:128]], axis=0), uzp, "tn")
             dv_ref[pair] = mm(wt, g, "tn")
             later_ref[pair] = later_gram
             later_ref[pairs + pair] = later_state

time: 220 us -> 201 us (0.914)
  Pallas kernels: 213 us -> 195 us
    pallas_call x3, Pallas kernels: 213 us -> 195 us  [call(): pl.pallas_call(body, out_shape=out_shape, in_specs=[vmem] * len(inputs),...]
where the time goes in v3:
time: 201 us
  Pallas kernels  195 us (97%)
  local copies, waits for them, and re-layouts  5.45 us (3%)
    pallas_call x3, Pallas kernels, call(): pl.pallas_call(body, out_shape=out_shape, in_specs=[vmem] * len(inputs),...  195 us
    unnamed x8, local copies, waits for them, and re-layouts  5.45 us

profile of v3, /device:TPU:0, one launch (start us, length us, event | category | flops | bytes accessed | tf_op | source)
XLA Modules:
  0.0 201.2 jit_solution(8770235329450937944)
XLA Ops:
  0.6 33.0 %shard_map.84 = (bf16[16,128,128]{2,1,0:T(8,128)(2,1)}, bf16[16,128,128]{2,1,0:T(8,128)(2,1)}, bf16[16,128,128]{2,1,0:T(8,128)(2,1)}, bf16[16,128,128]{2,1,0:T(8,128)(2,1)}, f32[8,128,128]{2,1,0:T(8,128)}) custom-call(bf16[16,128,128]{2,1,0:T(8,128)(2,1)} %q_in.1, bf16[16,128,128]{2,1,0:T(8,128)(2,1)} %k_in.1, bf16[16,128,128]{2,1,0:T(8,128)(2,1)} %v_in.1, ...), custom_call_target="tpu_custom_call" | custom-call | flops 1000000000 | bytes 8388608 | tf_op jit(solution)/shard_map/pallas_call | solution.py:497
  33.7 118.5 %shard_map.85 = (bf16[16,128,128]{2,1,0:T(8,128)(2,1)}, bf16[16,128,128]{2,1,0:T(8,128)(2,1)}, f32[16,128,128]{2,1,0:T(8,128)}, f32[16,128,128]{2,1,0:T(8,128)},...) custom-call(bf16[16,128,128]{2,1,0:T(8,128)(2,1)} %get-tuple-element.15.q_ref, ...), custom_call_target="tpu_custom_call" | custom-call | flops 1000000000 | bytes 8388608 | tf_op jit(solution)/shard_map/pallas_call | solution.py:497
  152.2 43.5 %shard_map.86 = (bf16[16,128,128]{2,1,0:T(8,128)(2,1)}, bf16[16,128,128]{2,1,0:T(8,128)(2,1)}, bf16[16,128,128]{2,1,0:T(8,128)(2,1)}, bf16[16,128,128]{2,1,0:T(8,128)(2,1)}) custom-call(bf16[16,128,128]{2,1,0:T(8,128)(2,1)} %get-tuple-element.20.o_in, bf16[16,128,128]{2,1,0:T(8,128)(2,1)} %get-tuple-element.21.dq_in, ...), custom_call_target="tpu_custom_call" | custom-call | flops 1000000000 | bytes 8388608 | tf_op jit(solution)/shard_map/pallas_call | solution.py:497
  195.7 0.0 copy-start.1
  195.7 0.0 copy-start
  195.7 2.0 copy.13
  197.7 1.9 copy.14
  199.6 0.0 copy-done.1
  199.6 0.8 copy.15
  200.4 0.0 copy-done
  200.4 0.8 copy.16
Async XLA Ops:
  195.7 3.9 %copy-start.1 = (bf16[16,128,128]{2,1,0:T(8,128)(2,1)S(1)}, bf16[16,128,128]{2,1,0:T(8,128)(2,1)}, u32[]{:S(2)}) copy-start(bf16[16,128,128]{2,1,0:T(8,128)(2,1)} %get-tuple-element.32) | copy-start | bytes 1572868
  195.7 4.7 %copy-start = (bf16[16,128,128]{2,1,0:T(8,128)(2,1)S(1)}, bf16[16,128,128]{2,1,0:T(8,128)(2,1)}, u32[]{:S(2)}) copy-start(bf16[16,128,128]{2,1,0:T(8,128)(2,1)} %get-tuple-element.33) | copy-start | bytes 1572868
